TPU v7x, 256 devices: a whole 4x4x8 slice. The times are simulated.
256 devices in a mesh: ctx: 32 (over y, x, core), ch: 8 (over z).
Axes of the slice: x: 4, y: 4, z: 8, core: 2. Of those that a mesh axis runs over, the one named last changes fastest.
Arguments:
- queries: bfloat16 [16384, 128], P('ctx'), may hold values from -6 to 6
- codes: int32 [16384], P('ctx'), may hold values from 0 to 511
- codebook: bfloat16 [512, 128], replicated, may hold values from -6 to 6
- values: bfloat16 [16384, 4096], P('ctx', 'ch'), may hold values from -6 to 6
- grad_out: bfloat16 [16384, 4096], P('ctx', 'ch'), may hold values from -0.75 to 0.75
- attn_out: bfloat16 [16384, 4096], P('ctx', 'ch'), may hold values from -6 to 6
- normalizer: float32 [16384], P('ctx'), as said below
Outputs:
- grad_values: bfloat16 [16384, 4096], P('ctx', 'ch')
- grad_queries: float32 [16384, 128], P('ctx')
- grad_codebook: float32 [512, 128], replicated
Inputs may be any that keep to these rules, and one draw needn't show every extreme that they name: normalizer[t] lies within 0.3 of 0.5 ln(1 + t); it is used as given and is not recomputed from the scores.
All inputs are finite; a program needn't handle non-finite values.
Results may differ from a plain program's by a relative error of at most 0.0057.
Values sent between devices are 32-bit elements; how exact they have to be, the bound alone decides.
A program may use at most 192 MiB of HBM per device.

v0:
```python
import jax
import jax.numpy as jnp
from jax import lax
from jax.sharding import PartitionSpec as P

DK = 128
BLOCK = 512


def carried_in(value, axis, join, neutral, backward):
    count, mine = (lax.axis_size(axis), lax.axis_index(axis))
    pieces = jax.tree.map(lambda part: lax.all_gather(part, axis), value)
    if backward:
        pieces = jax.tree.map(lambda part: part[::-1], pieces)
        mine = count - 1 - mine
    total = jax.tree.map(
        lambda part, zero: jnp.full_like(part, 0) + jnp.asarray(zero, part.dtype), value, neutral
    )

    def lap(position, total):
        longer = join(total, jax.tree.map(lambda part: part[position], pieces))
        return jax.tree.map(lambda new, old: jnp.where(position < mine, new, old), longer, total)

    return lax.fori_loop(0, count - 1, lap, total)


def add_pair(earlier, later):
    return (earlier[0] + later[0], earlier[1] + later[1])


def add_terms(earlier, later):
    return earlier + later


def take_rows(table, indices):
    return jnp.take(table, indices, axis=0)


def code_grads(
    in_block,
    code_weight,
    cross_sum,
    cached_sum,
    delta_sum,
    onehot_blocks,
    count_blocks,
    row_start,
    row_count,
):
    span = min(row_count, BLOCK)
    groups = row_count // span
    block_ids = (row_start + jnp.arange(groups, dtype=jnp.int32) * span) // BLOCK
    probs = in_block.reshape(groups, span, BLOCK)
    weights = code_weight.reshape(groups, span, -1)
    onehot_pick = jnp.take(onehot_blocks, block_ids, axis=0)
    count_pick = jnp.take(count_blocks, block_ids, axis=0)
    delta_rows = delta_sum.reshape(groups, span, 1)
    dscore = probs * (cross_sum.reshape(groups, span, BLOCK) - delta_rows)
    gathered = jnp.einsum(
        "gml,gls->gms",
        dscore,
        onehot_pick,
        precision=lax.Precision.HIGHEST,
        preferred_element_type=jnp.float32,
    )
    grads = (
        weights * (cached_sum.reshape(groups, span, -1) - count_pick[:, None, :] * delta_rows)
        + gathered
    )
    return grads.reshape(row_count, -1).astype(jnp.bfloat16)


def local(queries, codes, codebook, values, grad_out, attn_out, normalizer):
    tokens_here = queries.shape[0]
    channels = values.shape[1]
    code_count = codebook.shape[0]
    block_count = tokens_here // BLOCK
    score_scale = DK ** (-0.5)
    code_ids = jnp.arange(code_count, dtype=jnp.int32)
    onehot = codes[:, None] == code_ids[None, :]
    onehot_half = onehot.astype(jnp.bfloat16).reshape(block_count, BLOCK, code_count)
    onehot_full = onehot.astype(jnp.float32).reshape(block_count, BLOCK, code_count)
    code_blocks = codes.reshape(block_count, BLOCK)
    keys = jnp.take(codebook, codes, axis=0).reshape(block_count, BLOCK, -1)
    query_blocks = queries.reshape(block_count, BLOCK, -1)
    value_blocks = values.reshape(block_count, BLOCK, channels)
    grad_blocks = grad_out.reshape(block_count, BLOCK, channels)
    out_blocks = attn_out.reshape(block_count, BLOCK, channels)
    norm_blocks = normalizer.reshape(block_count, BLOCK)
    code_sums = jnp.einsum(
        "bls,blc->bsc", onehot_half, value_blocks, preferred_element_type=jnp.float32
    )
    code_tally = jnp.sum(onehot_full, axis=1)
    empty_sums = jnp.zeros((code_count, channels), jnp.float32)
    empty_tally = jnp.zeros((code_count,), jnp.float32)
    before, before_tally = carried_in(
        (jnp.sum(code_sums, axis=0), jnp.sum(code_tally, axis=0)),
        "ctx",
        add_pair,
        (empty_sums, empty_tally),
        False,
    )
    running = jnp.concatenate(
        [jnp.zeros_like(code_sums), jnp.cumsum(code_sums, axis=0)[:-1]], axis=0
    )
    running_tally = jnp.concatenate(
        [jnp.zeros_like(code_tally), jnp.cumsum(code_tally, axis=0)[:-1]], axis=0
    )
    totals = before[None] + running
    count_blocks = before_tally[None] + running_tally
    positions = jnp.arange(BLOCK, dtype=jnp.int32)
    causal = positions[:, None] >= positions[None, :]
    logits = (
        jnp.einsum("bld,bmd->blm", query_blocks, keys, preferred_element_type=jnp.float32)
        * score_scale
    )
    in_block = jnp.where(causal[None], jnp.exp(logits - norm_blocks[..., None]), 0.0)
    code_logits = (
        jnp.einsum("bld,sd->bls", query_blocks, codebook, preferred_element_type=jnp.float32)
        * score_scale
    )
    code_weight = jnp.exp(code_logits - norm_blocks[..., None])
    row_delta = jnp.sum(
        grad_blocks.astype(jnp.float32) * out_blocks.astype(jnp.float32), axis=2
    ).reshape(tokens_here)
    cross = jnp.einsum(
        "bld,bmd->blm", grad_blocks, value_blocks, preferred_element_type=jnp.float32
    )
    cached = jnp.einsum(
        "blc,bsc->bls", grad_blocks, totals.astype(jnp.bfloat16), preferred_element_type=jnp.float32
    )
    block_grad = jnp.einsum(
        "bls,blc->bsc",
        code_weight.astype(jnp.bfloat16),
        grad_blocks,
        preferred_element_type=jnp.float32,
    )
    later = carried_in(jnp.sum(block_grad, axis=0), "ctx", add_terms, empty_sums, True)
    inclusive = jnp.cumsum(block_grad[::-1], axis=0)[::-1]
    exclusive = jnp.concatenate([inclusive[1:], jnp.zeros_like(block_grad)], axis=0)
    later_grad = later[None] + exclusive
    looked_up = jax.vmap(take_rows)(later_grad, code_blocks)
    grad_values = (
        jnp.einsum(
            "blm,blc->bmc",
            in_block.astype(jnp.bfloat16),
            grad_blocks,
            preferred_element_type=jnp.float32,
        )
        + looked_up
    ).astype(jnp.bfloat16)
    grad_values = grad_values.reshape(tokens_here, channels)
    block_rows = in_block.reshape(tokens_here, BLOCK)
    weight_rows = code_weight.reshape(tokens_here, code_count)
    cross_rows = cross.reshape(tokens_here, BLOCK)
    cached_rows = cached.reshape(tokens_here, code_count)
    cross_sum, cached_sum, delta_sum = lax.psum((cross_rows, cached_rows, row_delta), "ch")
    row_start = 0
    code_grad = code_grads(
        block_rows,
        weight_rows,
        cross_sum,
        cached_sum,
        delta_sum,
        onehot_full,
        count_blocks,
        row_start,
        tokens_here,
    )
    query_grad = jnp.dot(code_grad, codebook, preferred_element_type=jnp.float32) * score_scale
    book_part = jnp.dot(code_grad.T, queries, preferred_element_type=jnp.float32) * score_scale
    grad_codebook = lax.psum(book_part, "ctx")
    return (grad_values, query_grad, grad_codebook)


def solution(mesh):
    in_specs = (
        P("ctx", None),
        P("ctx"),
        P(),
        P("ctx", "ch"),
        P("ctx", "ch"),
        P("ctx", "ch"),
        P("ctx"),
    )
    out_specs = (P("ctx", "ch"), P("ctx", None), P())
    return jax.shard_map(local, mesh=mesh, in_specs=in_specs, out_specs=out_specs, check_vma=False)
```

profile of v0, /device:TPU:1, one launch (start us, length us, event | category | flops | bytes accessed | tf_op | source)
XLA Modules:
  0.0 482.2 jit_solution(2487977797425039672)
XLA Ops:
  8.2 2.2 fusion.11
  12.7 2.5 fusion.17
  16.2 25.8 %all-gather.3 = f32[32,1,512]{2,1,0:T(1,128)S(1)} all-gather(f32[1,1,512]{2,1,0:T(1,128)S(1)} %bitcast.51), channel_id=4, replica_groups=mesh['ctx'=32,'ch'=8] {'ctx'}, dimensions={0}, use_global_device_ids=true | all-gather | bytes 67584 | tf_op jit(solution)/shard_map/all_gather | solution.py:12
  42.7 2.0 gather_fusion
  46.1 16.2 %psum.29 = f32[512]{0:T(512)S(1)} all-reduce(f32[512]{0:T(512)S(1)} %multiply_reduce_fusion), channel_id=1, replica_groups=mesh['ctx'=32,'ch'=8] {'ch'}, use_global_device_ids=true, to_apply=%region_7.8 | all-reduce | flops 512 | bytes 4096 | tf_op jit(solution)/shard_map/psum | solution.py:157
  63.1 2.3 fusion.3
  65.4 2.5 fusion.27
  67.8 65.9 %all-gather.9.cloned.1.call-done = f32[16384,512]{1,0:T(8,128)} async-done(((f32[512,512]{1,0:T(8,128)}), f32[16384,512]{1,0:T(8,128)}) %all-gather.9.cloned.1.call-update) | async-done | bytes 33554448 | tf_op jit(solution)/shard_map/all_gather | solution.py:12
  133.8 52.3 %while.31 = (s32[]{:T(128)}, f32[512,512]{1,0:T(8,128)S(1)}, f32[512]{0:T(512)S(1)}, s32[]{:T(128)}, f32[32,512,512]{2,1,0:T(8,128)}, /*index=5*/f32[32,512]{1,0:T(8,128)S(1)}, s32[]{:T(128)}, s32[]{:T(128)}) while((s32[]{:T(128)}, f32[512,512]{1,0:T(8,128)S(1)}, f32[512]{0:T(512)S(1)}, s32[]{:T(128)}, f32[32,512,512]{2,1,0:T(8,128)}, ...), condition=%wide.region_4.5_spmd.clone, body=%wide.region_3.4_spmd.clone.sunk | while | flops 787972 | bytes 3156083 | solution.py:24
  135.4 1.6 add_select_fusion.7
  137.1 1.6 add_select_fusion.7
  138.7 1.6 add_select_fusion.7
  140.4 1.6 add_select_fusion.7
  142.0 1.6 add_select_fusion.7
  143.7 1.6 add_select_fusion.7
  145.4 1.6 add_select_fusion.7
  147.0 1.7 add_select_fusion.7
  148.8 1.7 add_select_fusion.7
  150.5 1.6 add_select_fusion.7
  152.2 1.6 add_select_fusion.7
  153.8 1.6 add_select_fusion.7
  155.5 1.6 add_select_fusion.7
  157.2 1.6 add_select_fusion.7
  158.9 1.6 add_select_fusion.7
  160.5 1.6 add_select_fusion.7
  162.2 1.6 add_select_fusion.7
  163.9 1.6 add_select_fusion.7
  165.6 1.6 add_select_fusion.7
  167.2 1.6 add_select_fusion.7
  168.9 1.6 add_select_fusion.7
  170.5 1.6 add_select_fusion.7
  172.2 1.6 add_select_fusion.7
  173.8 1.6 add_select_fusion.7
  175.5 1.6 add_select_fusion.7
  177.1 1.6 add_select_fusion.7
  178.8 1.6 add_select_fusion.7
  180.5 1.9 add_select_fusion.7
  182.4 1.9 add_select_fusion.7
  184.4 1.6 add_select_fusion.7
  186.0 2.5 convolution_bitcast_fusion
  188.5 66.0 %all-gather.7.cloned.1.call-done = f32[16384,512]{1,0:T(8,128)} async-done(((f32[512,512]{1,0:T(8,128)}), f32[16384,512]{1,0:T(8,128)}) %all-gather.7.cloned.1.call-update) | async-done | bytes 33554448 | tf_op jit(solution)/shard_map/all_gather | solution.py:12
  254.6 23.3 %rev.3 = f32[32,512,512]{2,1,0:T(8,128)} reverse(f32[32,512,512]{2,1,0:T(8,128)} %bitcast.46), dimensions={0} | reverse | bytes 67108864 | tf_op jit(solution)/shard_map/rev | solution.py:14
  278.0 50.3 %while.30 = (s32[]{:T(128)}, f32[512,512]{1,0:T(8,128)S(1)}, s32[]{:T(128)}, f32[32,512,512]{2,1,0:T(8,128)}, s32[]{:T(128)}, /*index=5*/s32[]{:T(128)}) while((s32[]{:T(128)}, f32[512,512]{1,0:T(8,128)S(1)}, s32[]{:T(128)}, f32[32,512,512]{2,1,0:T(8,128)}, s32[]{:T(128)}, /*index=5*/s32[]{:T(128)}) %tuple.63), condition=%wide.region_1.2_spmd.clone, body=%wide.region_0.1_spmd.clone.sunk | while | flops 786436 | bytes 3145821 | solution.py:24
  278.0 1.6 add_select_fusion.6
  287.7 1.6 add_select_fusion.6
  292.6 1.6 add_select_fusion.6
  294.2 1.6 add_select_fusion.6
  295.8 1.6 add_select_fusion.6
  297.5 1.6 add_select_fusion.6
  299.1 1.6 add_select_fusion.6
  302.3 1.6 add_select_fusion.6
  304.0 1.6 add_select_fusion.6
  305.6 1.6 add_select_fusion.6
  307.2 1.6 add_select_fusion.6
  308.8 1.6 add_select_fusion.6
  310.5 1.6 add_select_fusion.6
  312.1 1.6 add_select_fusion.6
  313.7 1.6 add_select_fusion.6
  328.3 5.5 %gather_fusion.1 = f32[512,512]{1,0:T(8,128)} fusion(f32[1,512,512]{2,1,0:T(8,128)S(1)} %bitcast.44, s32[512]{0:T(512)S(1)} %bitcast.45), kind=kCustom, calls=%fused_computation.1 | custom fusion | bytes 2101248 | tf_op jit(solution)/shard_map/vmap(jit(_take))/gather | solution.py:36
  333.8 2.8 fusion.7
  336.6 19.5 %all-reduce.6.cloned.1.call-done = (f32[512,512]{0,1:T(8,128)}, f32[512,512]{0,1:T(8,128)}) async-done(((f32[512,512]{0,1:T(8,128)}, f32[512,512]{0,1:T(8,128)}), (f32[512,512]{0,1:T(8,128)}, f32[512,512]{0,1:T(8,128)})) %all-reduce.6.cloned.1.call-update) | async-done | bytes 2097168 | tf_op jit(solution)/shard_map/psum | solution.py:157
  356.1 3.2 fusion.6
  361.4 112.6 %all-reduce.4.cloned.1.call-done = f32[512,128]{1,0:T(8,128)} async-done(((f32[512,128]{1,0:T(8,128)}), f32[512,128]{1,0:T(8,128)}) %all-reduce.4.cloned.1.call-update) | async-done | bytes 262160 | tf_op jit(solution)/shard_map/psum | solution.py:172
  474.0 1.7 copy.48
  (117 shorter events, 37.1 us)
Async XLA Ops:
  7.2 1.1 copy-start
  7.2 126.6 %all-gather.9.cloned.1.call-start = ((), (), s32[]{:S(2)}) async-start(), calls=%async_computation.2 | async-start | bytes 34603008 | tf_op jit(solution)/shard_map/all_gather | solution.py:12
  10.4 244.1 %all-gather.7.cloned.1.call-start = ((), (), s32[]{:S(2)}) async-start(), calls=%async_computation.1 | async-start | bytes 34603008 | tf_op jit(solution)/shard_map/all_gather | solution.py:12
  11.8 1.0 copy-start.4
  15.2 340.8 %all-reduce.6.cloned.1.call-start = ((), (), s32[]{:S(2)}) async-start(), calls=%async_computation.3 | async-start | bytes 4194304 | tf_op jit(solution)/shard_map/psum | solution.py:157
  254.6 79.2 %copy-start.2 = (bf16[512,512]{1,0:T(8,128)(2,1)S(1)}, bf16[512,512]{1,0:T(8,128)(2,1)}, u32[]{:S(2)}) copy-start(bf16[512,512]{1,0:T(8,128)(2,1)} %param.15) | copy-start | bytes 1572868
  254.6 101.5 %copy-start.5 = (f32[512,512]{0,1:T(8,128)S(1)}, f32[512,512]{0,1:T(8,128)}, u32[]{:S(2)}) copy-start(f32[512,512]{0,1:T(8,128)} %copy-done.4) | copy-start | bytes 3145732
  254.6 101.5 %copy-start.7 = (s32[512]{0:T(512)S(1)}, s32[512]{0:T(512)}, u32[]{:S(2)}) copy-start(s32[512]{0:T(512)} %param.12) | copy-start | bytes 6148
  254.6 221.1 %copy-start.1 = (bf16[512,512]{1,0:T(8,128)(2,1)S(1)}, bf16[512,512]{1,0:T(8,128)(2,1)}, u32[]{:S(2)}) copy-start(bf16[512,512]{1,0:T(8,128)(2,1)} %param.14) | copy-start | bytes 1572868
  277.9 81.4 %copy-start.6 = (bf16[512,128]{1,0:T(8,128)(2,1)S(1)}, bf16[512,128]{1,0:T(8,128)(2,1)}, u32[]{:S(2)}) copy-start(bf16[512,128]{1,0:T(8,128)(2,1)} %param.11) | copy-start | bytes 393220
  277.9 82.4 %copy-start.3 = (bf16[512,128]{1,0:T(8,128)(2,1)S(1)}, bf16[512,128]{1,0:T(8,128)(2,1)}, u32[]{:S(2)}) copy-start(bf16[512,128]{1,0:T(8,128)(2,1)} %param.13) | copy-start | bytes 393220
  277.9 196.0 %all-reduce.4.cloned.1.call-start = ((), (), s32[]{:S(2)}) async-start(), calls=%async_computation | async-start | bytes 524288 | tf_op jit(solution)/shard_map/psum | solution.py:172
Sparse Core Ops, SparseCore 0:
  10.6 123.1 all-gather.8
  136.3 118.1 all-gather.6
  278.1 77.9 all-reduce.5
  360.5 113.4 all-reduce.3
where the time goes:
time: 485 us; the launch traced here: 482 us
  waiting for transfers between devices  264 us (54%)
  other arithmetic  104 us (21%)
  blocking collectives  42.1 us (9%)
  local copies, waits for them, and re-layouts  34.9 us (7%)
  matrix products  21.3 us (4%)
  between operations  13.9 us (3%)
    all_gather x2, waiting for transfers between devices, carried_in(): pieces = jax.tree.map(lambda part: lax.all_gather(part, axis), value)  132 us
    psum x1, waiting for transfers between devices, local(): grad_codebook = lax.psum(book_part, 'ctx')  113 us
    select_n x93, other arithmetic, lap(): jnp.where(position < mine, new, old)  100 us
    all_gather x1, blocking collectives, carried_in(): pieces = jax.tree.map(lambda part: lax.all_gather(part, axis), value)  25.8 us
    rev x1, local copies, waits for them, and re-layouts, carried_in(): pieces = jax.tree.map(lambda part: part[::-1], pieces)  23.3 us
    psum x1, waiting for transfers between devices, local(): lax.psum((cross_rows, cached_rows, row_delta), 'ch')  19.5 us
    psum x1, blocking collectives, local(): lax.psum((cross_rows, cached_rows, row_delta), 'ch')  16.2 us
  transfers between devices with their start and end apart: 4, of which 4 were waited for; matrix products, arithmetic and copies ran while one was open for 26% of the time, Pallas kernels for 0%

commit v1 on v0

v1 whole, which is shorter than its diff:
```python
import functools

import jax
import jax.numpy as jnp
from jax import lax
from jax.experimental import pallas as pl
from jax.experimental.pallas import tpu as pltpu
from jax.sharding import PartitionSpec as P

MESH = pl.DeviceIdType.MESH
F32 = jnp.float32
BF16 = jnp.bfloat16

NN = (((1,), (0,)), ((), ()))
NT = (((1,), (1,)), ((), ()))


def dot(a, b, dims=NN):
    return lax.dot_general(a, b, dims, preferred_element_type=F32)


def split(x):
    high = x.astype(BF16)
    return high, (x - high.astype(F32)).astype(BF16)


def kernel(
    chips,
    depth,
    codes_ref,
    norm_ref,
    query_ref,
    book_ref,
    value_ref,
    grad_ref,
    out_ref,
    gv_ref,
    gq_ref,
    gb_ref,
    onehot,
    weight,
    probs,
    inner,
    local_values,
    sums,
    sums_x,
    sums_t,
    sums_in,
    sums_out,
    sums_p,
    sums_f,
    sums_h,
    grads,
    grads_x,
    grads_t,
    grads_in,
    grads_out,
    grads_p,
    grads_f,
    grads_h,
    tally,
    tally_x,
    tally_t,
    tally_in,
    book_p,
    book_x,
    book_t,
    book_in,
    book_s,
    book_z,
    book_o,
    book_r,
    book_h,
    gq_p,
    gq_in,
    gq_s,
    gq_r,
    core_send,
    core_recv,
    plane_send,
    plane_recv,
    z_send,
    z_recv,
):
    tokens, channels = value_ref.shape
    codes, dk = book_ref.shape
    half = codes // 2
    piece = half // chips
    zrows = dk // depth
    scale = float(dk) ** -0.5

    ctx = lax.axis_index("ctx")
    z = lax.axis_index("ch")
    chip = ctx // 2
    core = lax.rem(ctx, 2)
    other = chip * 2 + (1 - core)
    is_one = core.astype(F32)
    is_zero = 1.0 - is_one
    mine = pl.ds(pl.multiple_of(core * half, half), half)
    theirs = pl.ds(pl.multiple_of((1 - core) * half, half), half)

    def rows(k, size):
        return pl.ds(pl.multiple_of(k * size, size), size)

    def core_copy(n, src, dst):
        return pltpu.make_async_remote_copy(
            src_ref=src,
            dst_ref=dst,
            send_sem=core_send.at[n],
            recv_sem=core_recv.at[n],
            device_id={"ctx": other},
            device_id_type=MESH,
        )

    def plane_copy(n, k, src, dst, slot):
        return pltpu.make_async_remote_copy(
            src_ref=src,
            dst_ref=dst,
            send_sem=plane_send.at[n, k],
            recv_sem=plane_recv.at[n, slot],
            device_id={"ctx": k * 2 + core},
            device_id_type=MESH,
        )

    def z_copy(n, k, src, dst, slot):
        return pltpu.make_async_remote_copy(
            src_ref=src,
            dst_ref=dst,
            send_sem=z_send.at[n, k],
            recv_sem=z_recv.at[n, slot],
            device_id={"ch": k},
            device_id_type=MESH,
        )

    def over_plane(body):
        def step(i, carry):
            body(lax.rem(chip + i, chips))
            return carry

        lax.fori_loop(1, chips, step, 0)

    def over_z(body):
        def step(i, carry):
            body(lax.rem(z + i, depth))
            return carry

        lax.fori_loop(1, depth, step, 0)

    barrier = pltpu.get_barrier_semaphore()
    pl.semaphore_signal(barrier, inc=1, device_id={"ctx": other}, device_id_type=MESH)
    over_plane(
        lambda k: pl.semaphore_signal(
            barrier, inc=1, device_id={"ctx": k * 2 + core}, device_id_type=MESH
        )
    )
    over_z(lambda k: pl.semaphore_signal(barrier, inc=1, device_id={"ch": k}, device_id_type=MESH))

    code_row = codes_ref[...]
    onehot[...] = jnp.where(
        lax.broadcasted_iota(jnp.int32, (codes, tokens), 0) == code_row, 1.0, 0.0
    ).astype(BF16)
    sums[...] = dot(onehot[...], value_ref[...])
    tally[...] = dot(jnp.ones((8, tokens), BF16), onehot[...], NT)

    pl.semaphore_wait(barrier, 1 + (chips - 1) + (depth - 1))

    s_core = core_copy(0, sums.at[theirs], sums_x)
    s_core.start()
    t_core = core_copy(1, tally, tally_x)
    t_core.start()

    norm_row = norm_ref[...]
    weight[...] = jnp.exp(dot(book_ref[...], query_ref[...], NT) * scale - norm_row)
    grads[...] = dot(weight[...].astype(BF16), grad_ref[...])
    g_core = core_copy(2, grads.at[theirs], grads_x)
    g_core.start()

    s_core.wait_recv()
    sums_t[...] = sums[mine] + sums_x[...]
    over_plane(
        lambda k: plane_copy(0, k, sums_t.at[rows(k, piece)], sums_in.at[chip], chip).start()
    )
    sums_in[chip] = sums_t[rows(chip, piece)]
    t_core.wait_recv()
    tally_t[...] = tally[...] + tally_x[...]
    over_plane(lambda k: plane_copy(1, k, tally_t, tally_in.at[chip], chip).start())
    tally_in[chip] = tally_t[...]

    g_core.wait_recv()
    grads_t[...] = grads[mine] + grads_x[...]
    over_plane(
        lambda k: plane_copy(2, k, grads_t.at[rows(k, piece)], grads_in.at[chip], chip).start()
    )
    grads_in[chip] = grads_t[rows(chip, piece)]

    key_t = dot(book_ref[...].astype(F32).T.astype(BF16), onehot[...]).astype(BF16)
    keys = key_t.astype(F32).T.astype(BF16)
    causal = lax.broadcasted_iota(jnp.int32, (tokens, tokens), 0) <= lax.broadcasted_iota(
        jnp.int32, (tokens, tokens), 1
    )
    in_block = jnp.where(
        causal, jnp.exp(dot(keys, query_ref[...], NT) * scale - norm_row), 0.0
    )
    probs[...] = in_block.astype(BF16)
    product = grad_ref[...].astype(F32) * out_ref[...].astype(F32)
    product_high, product_low = split(product)
    ones = jnp.ones((8, channels), BF16)
    delta = (dot(ones, product_high, NT) + dot(ones, product_low, NT))[0:1]
    dscore = in_block * (dot(value_ref[...], grad_ref[...], NT) - delta)
    dscore_high, dscore_low = split(dscore)
    inner[...] = dot(onehot[...], dscore_high) + dot(onehot[...], dscore_low)

    def wait_plane(n, buffer):
        over_plane(lambda k: plane_copy(n, k, buffer.at[k], buffer.at[k], k).wait_recv())

    def scan(buffer, result, backward):
        def step(i, total):
            k = chips - 1 - i if backward else i
            result[k] = total
            return total + buffer[k]

        lax.fori_loop(0, chips, step, jnp.zeros((piece, channels), F32))

    wait_plane(0, sums_in)
    scan(sums_in, sums_out, False)
    over_plane(
        lambda k: plane_copy(3, k, sums_out.at[k], sums_p.at[rows(chip, piece)], chip).start()
    )
    sums_p[rows(chip, piece)] = sums_out[chip]
    wait_plane(2, grads_in)
    scan(grads_in, grads_out, True)
    over_plane(
        lambda k: plane_copy(4, k, grads_out.at[k], grads_p.at[rows(chip, piece)], chip).start()
    )
    grads_p[rows(chip, piece)] = grads_out[chip]

    local_values[...] = dot(probs[...], grad_ref[...])

    wait_plane(1, tally_in)

    def count_step(k, total):
        return total + jnp.where(k < chip, 1.0, 0.0) * tally_in[k]

    count = lax.fori_loop(0, chips, count_step, is_one * tally_x[...])
    count_col = jnp.broadcast_to(count[0:1], (128, codes)).T[:, 0:1]

    def wait_rows(n, buffer, size):
        over_plane(
            lambda k: plane_copy(
                n, k, buffer.at[rows(k, size)], buffer.at[rows(k, size)], k
            ).wait_recv()
        )

    wait_rows(3, sums_p, piece)
    sums_f[...] = sums_p[...] + is_zero * sums[mine]
    s_back = core_copy(3, sums_f, sums_h)
    s_back.start()
    own_half = (sums_p[...] + is_one * sums_x[...]).astype(BF16)
    cached_own = dot(own_half, grad_ref[...], NT)
    cgrad_own = (
        weight[mine] * (cached_own - jnp.where(core == 1, count_col[half:], count_col[:half]) * delta)
        + inner[mine]
    )
    s_back.wait_recv()
    cached_other = dot(sums_h[...].astype(BF16), grad_ref[...], NT)
    cgrad_other = (
        weight[theirs]
        * (cached_other - jnp.where(core == 1, count_col[:half], count_col[half:]) * delta)
        + inner[theirs]
    )
    own_high, own_low = split(cgrad_own)
    other_high, other_low = split(cgrad_other)
    query = query_ref[...]
    book_p[0] = (dot(own_high, query) + dot(own_low, query)) * scale
    book_p[1] = (dot(other_high, query) + dot(other_low, query)) * scale
    b_core = core_copy(5, book_p.at[1], book_x)
    b_core.start()
    book_own = book_ref[mine].astype(F32).T.astype(BF16)
    book_other = book_ref[theirs].astype(F32).T.astype(BF16)
    gq_p[...] = (
        dot(book_own, own_high)
        + dot(book_own, own_low)
        + dot(book_other, other_high)
        + dot(book_other, other_low)
    ) * scale
    over_z(lambda k: z_copy(0, k, gq_p.at[rows(k, zrows)], gq_in.at[z], z).start())
    gq_in[z] = gq_p[rows(z, zrows)]

    b_core.wait_recv()
    book_t[...] = book_p[0] + book_x[...]
    over_plane(lambda k: plane_copy(5, k, book_t.at[rows(k, piece)], book_in.at[chip], chip).start())
    book_in[chip] = book_t[rows(chip, piece)]

    wait_rows(4, grads_p, piece)
    grads_f[...] = grads_p[...] + is_one * grads[mine]
    g_back = core_copy(4, grads_f, grads_h)
    g_back.start()

    wait_plane(5, book_in)
    book_s[...] = lax.fori_loop(
        0, chips, lambda k, total: total + book_in[k], jnp.zeros((piece, dk), F32)
    )
    over_z(lambda k: z_copy(1, k, book_s, book_z.at[z], z).start())
    book_z[z] = book_s[...]

    def wait_z(n, buffer):
        over_z(lambda k: z_copy(n, k, buffer.at[k], buffer.at[k], k).wait_recv())

    wait_z(0, gq_in)
    gq_s[...] = lax.fori_loop(
        0, depth, lambda k, total: total + gq_in[k], jnp.zeros((zrows, tokens), F32)
    )
    over_z(lambda k: z_copy(2, k, gq_s, gq_r.at[rows(z, zrows)], z).start())
    gq_r[rows(z, zrows)] = gq_s[...]

    wait_z(1, book_z)
    book_o[...] = lax.fori_loop(
        0, depth, lambda k, total: total + book_z[k], jnp.zeros((piece, dk), F32)
    )
    over_plane(lambda k: plane_copy(6, k, book_o, book_r.at[rows(chip, piece)], chip).start())
    book_r[rows(chip, piece)] = book_o[...]

    own_later = grads_p[...] + is_zero * grads_x[...]
    lookup = onehot[...].T
    low_half = core == 0
    g_back.wait_recv()
    other_later = grads_h[...]
    first = jnp.where(low_half, own_later, other_later)
    second = jnp.where(low_half, other_later, own_later)
    first_high, first_low = split(first)
    second_high, second_low = split(second)
    looked_up = (
        dot(lookup[:, :half], first_high)
        + dot(lookup[:, :half], first_low)
        + dot(lookup[:, half:], second_high)
        + dot(lookup[:, half:], second_low)
    )
    gv_ref[...] = (local_values[...] + looked_up).astype(BF16)

    wait_rows(6, book_r, piece)
    b_back = core_copy(6, book_r, book_h)
    b_back.start()
    over_z(
        lambda k: z_copy(2, k, gq_r.at[rows(k, zrows)], gq_r.at[rows(k, zrows)], k).wait_recv()
    )
    gq_ref[...] = gq_r[...].T
    gb_ref[mine] = book_r[...]
    b_back.wait_recv()
    gb_ref[theirs] = book_h[...]

    for copy in (s_core, t_core, g_core, s_back, b_core, g_back, b_back):
        copy.wait_send()

    def drain_plane(k):
        plane_copy(0, k, sums_t.at[rows(k, piece)], sums_in.at[chip], chip).wait_send()
        plane_copy(1, k, tally_t, tally_in.at[chip], chip).wait_send()
        plane_copy(2, k, grads_t.at[rows(k, piece)], grads_in.at[chip], chip).wait_send()
        plane_copy(3, k, sums_out.at[k], sums_p.at[rows(chip, piece)], chip).wait_send()
        plane_copy(4, k, grads_out.at[k], grads_p.at[rows(chip, piece)], chip).wait_send()
        plane_copy(5, k, book_t.at[rows(k, piece)], book_in.at[chip], chip).wait_send()
        plane_copy(6, k, book_o, book_r.at[rows(chip, piece)], chip).wait_send()

    def drain_z(k):
        z_copy(0, k, gq_p.at[rows(k, zrows)], gq_in.at[z], z).wait_send()
        z_copy(1, k, book_s, book_z.at[z], z).wait_send()
        z_copy(2, k, gq_s, gq_r.at[rows(z, zrows)], z).wait_send()

    over_plane(drain_plane)
    over_z(drain_z)


def local(chips, depth, queries, codes, codebook, values, grad_out, attn_out, normalizer):
    tokens, channels = values.shape
    count, dk = codebook.shape
    half = count // 2
    piece = half // chips
    zrows = dk // depth

    def f32(*shape):
        return pltpu.VMEM(shape, F32)

    def scan_scratch():
        return [
            f32(count, channels),
            f32(half, channels),
            f32(half, channels),
            f32(chips, piece, channels),
            f32(chips, piece, channels),
            f32(half, channels),
            f32(half, channels),
            f32(half, channels),
        ]

    scratch = (
        [
            pltpu.VMEM((count, tokens), BF16),
            f32(count, tokens),
            pltpu.VMEM((tokens, tokens), BF16),
            f32(count, tokens),
            f32(tokens, channels),
        ]
        + scan_scratch()
        + scan_scratch()
        + [f32(8, count), f32(8, count), f32(8, count), f32(chips, 8, count)]
        + [
            f32(2, half, dk),
            f32(half, dk),
            f32(half, dk),
            f32(chips, piece, dk),
            f32(piece, dk),
            f32(depth, piece, dk),
            f32(piece, dk),
            f32(half, dk),
            f32(half, dk),
        ]
        + [f32(dk, tokens), f32(depth, zrows, tokens), f32(zrows, tokens), f32(dk, tokens)]
        + [
            pltpu.SemaphoreType.DMA((7,)),
            pltpu.SemaphoreType.DMA((7,)),
            pltpu.SemaphoreType.DMA((7, chips)),
            pltpu.SemaphoreType.DMA((7, chips)),
            pltpu.SemaphoreType.DMA((3, depth)),
            pltpu.SemaphoreType.DMA((3, depth)),
        ]
    )
    return pl.pallas_call(
        functools.partial(kernel, chips, depth),
        out_shape=(
            jax.ShapeDtypeStruct((tokens, channels), BF16),
            jax.ShapeDtypeStruct((tokens, dk), F32),
            jax.ShapeDtypeStruct((count, dk), F32),
        ),
        in_specs=[pl.BlockSpec(memory_space=pltpu.VMEM)] * 7,
        out_specs=[pl.BlockSpec(memory_space=pltpu.VMEM)] * 3,
        scratch_shapes=scratch,
        compiler_params=pltpu.CompilerParams(
            collective_id=0, has_side_effects=True, vmem_limit_bytes=56 * 1024 * 1024
        ),
        name="vq_backward",
    )(
        codes.reshape(1, tokens),
        normalizer.reshape(1, tokens),
        queries,
        codebook,
        values,
        grad_out,
        attn_out,
    )


def solution(mesh):
    in_specs = (
        P("ctx", None),
        P("ctx"),
        P(),
        P("ctx", "ch"),
        P("ctx", "ch"),
        P("ctx", "ch"),
        P("ctx"),
    )
    out_specs = (P("ctx", "ch"), P("ctx", None), P())
    step = functools.partial(local, mesh.shape["ctx"] // 2, mesh.shape["ch"])
    return jax.shard_map(step, mesh=mesh, in_specs=in_specs, out_specs=out_specs, check_vma=False)
```

time: 485 us -> 67.6 us (0.14)
  waiting for transfers between devices: 264 us -> 0 us
  other arithmetic: 104 us -> 0 us
  Pallas kernels: 0 us -> 63.1 us
  blocking collectives: 42.1 us -> 0 us
  local copies, waits for them, and re-layouts: 34.9 us -> 3.66 us
  matrix products: 21.3 us -> 0 us
  between operations: 13.9 us -> 0.65 us
    psum x2 -> x0, waiting for transfers between devices: 132 us -> none  [the longest x1 113 us: local(): grad_codebook = lax.psum(book_part, 'ctx')]
    all_gather x2 -> x0, waiting for transfers between devices: 132 us -> none  [carried_in(): pieces = jax.tree.map(lambda part: lax.all_gather(part, axis), value)]
    select_n x94 -> x0, other arithmetic: 101 us -> none  [the longest x93 100 us: lap(): jnp.where(position < mine, new, old)]
    pallas_call x0 -> x1, Pallas kernels: none -> 63.1 us  [local(): pl.pallas_call(functools.partial(kernel, chips, depth), out_shape=(jax.Sh...]
    all_gather x1 -> x0, blocking collectives: 25.8 us -> none  [carried_in(): pieces = jax.tree.map(lambda part: lax.all_gather(part, axis), value)]
    rev x1 -> x0, local copies, waits for them, and re-layouts: 23.3 us -> none  [carried_in(): pieces = jax.tree.map(lambda part: part[::-1], pieces)]
    dot_general x10 -> x0, matrix products: 21.3 us -> none  [the longest x1 3.25 us: code_grads(): jnp.einsum('gml,gls->gms', dscore, onehot_pick, precision=lax.Precision.H...]
    psum x1 -> x0, blocking collectives: 16.2 us -> none  [local(): lax.psum((cross_rows, cached_rows, row_delta), 'ch')]
  transfers between devices with their start and end apart: 4 -> 0, of which waited for: 4 -> 0; matrix products, arithmetic and copies ran while one was open for 26% -> 0% of each run, Pallas kernels for 0% -> 0%
where the time goes in v1:
time: 67.6 us; the launch traced here: 67.4 us
  Pallas kernels  63.1 us (93%)
  local copies, waits for them, and re-layouts  3.66 us (5%)
    pallas_call x1, Pallas kernels, local(): pl.pallas_call(functools.partial(kernel, chips, depth), out_shape=(jax.Sh...  63.1 us
    unnamed x7, local copies, waits for them, and re-layouts  3.66 us

profile of v1, /device:TPU:1, one launch (start us, length us, event | category | flops | bytes accessed | tf_op | source)
XLA Modules:
  0.0 67.4 jit_solution(4359189964652851801)
XLA Ops:
  0.6 63.1 %vq_backward.1 = (bf16[512,512]{1,0:T(8,128)(2,1)}, f32[512,128]{1,0:T(8,128)}, f32[512,128]{1,0:T(8,128)}) custom-call(s32[1,512]{1,0:T(1,128)} %bitcast.2, f32[1,512]{1,0:T(1,128)} %bitcast.3, bf16[512,128]{1,0:T(8,128)(2,1)} %query_ref.1, bf16[512,128]{1,0:T(8,128)(2,1)} %book_ref.1, bf16[512,512]{1,0:T(8,128)(2,1)} %value_ref.1, ...), custom_call_target="tpu_custom_call" | custom-call | tf_op jit(solution)/shard_map/vq_backward/pallas_call | solution.py:426
  63.8 0.0 copy-start.1
  63.8 1.9 %copy.13 = bf16[512,512]{1,0:T(8,128)(2,1)} copy(bf16[512,512]{1,0:T(8,128)(2,1)} %get-tuple-element.6) | data formatting | bytes 1048576
  65.7 0.0 copy-done.1
  65.7 0.0 copy-start
  65.7 0.7 %copy.14 = f32[512,128]{1,0:T(8,128)} copy(f32[512,128]{1,0:T(8,128)S(1)} %copy-done.1) | data formatting | bytes 524288
  66.4 0.3 copy-done
  66.7 0.7 %copy.15 = f32[512,128]{1,0:T(8,128)} copy(f32[512,128]{1,0:T(8,128)S(1)} %copy-done) | data formatting | bytes 524288
Async XLA Ops:
  63.8 1.9 %copy-start.1 = (f32[512,128]{1,0:T(8,128)S(1)}, f32[512,128]{1,0:T(8,128)}, u32[]{:S(2)}) copy-start(f32[512,128]{1,0:T(8,128)} %get-tuple-element.7) | copy-start | bytes 786436
  65.7 1.0 %copy-start = (f32[512,128]{1,0:T(8,128)S(1)}, f32[512,128]{1,0:T(8,128)}, u32[]{:S(2)}) copy-start(f32[512,128]{1,0:T(8,128)} %get-tuple-element.8) | copy-start | bytes 786436

commit v2 on v1

v2 whole, which is shorter than its diff:
```python
import functools

import jax
import jax.numpy as jnp
from jax import lax
from jax.experimental import pallas as pl
from jax.experimental.pallas import tpu as pltpu
from jax.sharding import PartitionSpec as P

MESH = pl.DeviceIdType.MESH
EARLY = 8
F32 = jnp.float32
BF16 = jnp.bfloat16

FAR_FIRST = (
    ((2, 2), (2, 1), (1, 2), (2, 3), (3, 2), (1, 1), (1, 3), (3, 1), (3, 3), (2, 0), (0, 2))
    + ((1, 0), (3, 0), (0, 1), (0, 3))
)

NN = (((1,), (0,)), ((), ()))
NT = (((1,), (1,)), ((), ()))


def dot(a, b, dims=NN):
    return lax.dot_general(a, b, dims, preferred_element_type=F32)


def split(x):
    high = x.astype(BF16)
    return high, (x - high.astype(F32)).astype(BF16)


def kernel(
    chips,
    depth,
    codes_hbm,
    value_hbm,
    book_hbm,
    query_hbm,
    norm_hbm,
    grad_hbm,
    out_hbm,
    gv_ref,
    gq_ref,
    gb_ref,
    codes_ref,
    value_ref,
    book_ref,
    query_ref,
    norm_ref,
    grad_ref,
    out_ref,
    load_sem,
    onehot,
    weight,
    probs,
    inner,
    local_values,
    sums,
    sums_x,
    sums_t,
    sums_in,
    sums_out,
    sums_p,
    sums_f,
    sums_h,
    grads,
    grads_x,
    grads_t,
    grads_in,
    grads_out,
    grads_p,
    grads_f,
    grads_h,
    tally,
    tally_x,
    tally_t,
    tally_in,
    book_p,
    book_x,
    book_t,
    book_in,
    book_s,
    book_z,
    book_o,
    book_r,
    book_h,
    gq_p,
    gq_in,
    gq_s,
    gq_r,
    core_send,
    core_recv,
    plane_send,
    plane_recv,
    z_send,
    z_recv,
):
    tokens, channels = value_ref.shape
    codes, dk = book_ref.shape
    half = codes // 2
    piece = half // chips
    zrows = dk // depth
    early = EARLY
    scale = float(dk) ** -0.5

    ctx = lax.axis_index("ctx")
    z = lax.axis_index("ch")
    chip = ctx // 2
    core = lax.rem(ctx, 2)
    other = chip * 2 + (1 - core)
    is_one = core.astype(F32)
    is_zero = 1.0 - is_one
    mine = pl.ds(pl.multiple_of(core * half, half), half)
    theirs = pl.ds(pl.multiple_of((1 - core) * half, half), half)

    def rows(k, size):
        return pl.ds(pl.multiple_of(k * size, size), size)

    def core_copy(n, src, dst):
        return pltpu.make_async_remote_copy(
            src_ref=src,
            dst_ref=dst,
            send_sem=core_send.at[n],
            recv_sem=core_recv.at[n],
            device_id={"ctx": other},
            device_id_type=MESH,
        )

    def plane_copy(n, k, src, dst):
        return pltpu.make_async_remote_copy(
            src_ref=src,
            dst_ref=dst,
            send_sem=plane_send.at[n],
            recv_sem=plane_recv.at[n],
            device_id={"ctx": k * 2 + core},
            device_id_type=MESH,
        )

    def z_copy(n, k, src, dst):
        return pltpu.make_async_remote_copy(
            src_ref=src,
            dst_ref=dst,
            send_sem=z_send.at[n],
            recv_sem=z_recv.at[n],
            device_id={"ch": k},
            device_id_type=MESH,
        )

    def over_plane(body):
        def step(i, carry):
            body(lax.rem(chip + i, chips))
            return carry

        lax.fori_loop(1, chips, step, 0)

    def far_first(body):
        y, x = chip // 4, lax.rem(chip, 4)
        for dy, dx in FAR_FIRST:
            body(lax.rem(y + dy, 4) * 4 + lax.rem(x + dx, 4))

    def over_z(body):
        def step(i, carry):
            body(lax.rem(z + i, depth))
            return carry

        lax.fori_loop(1, depth, step, 0)

    loads = [
        pltpu.make_async_copy(source, target, load_sem.at[n])
        for n, (source, target) in enumerate(
            (
                (codes_hbm, codes_ref),
                (value_hbm, value_ref),
                (book_hbm, book_ref),
                (query_hbm, query_ref),
                (norm_hbm, norm_ref),
                (grad_hbm, grad_ref),
                (out_hbm, out_ref),
            )
        )
    ]
    for load in loads:
        load.start()

    barrier = pltpu.get_barrier_semaphore()
    pl.semaphore_signal(barrier, inc=1, device_id={"ctx": other}, device_id_type=MESH)
    over_plane(
        lambda k: pl.semaphore_signal(
            barrier, inc=1, device_id={"ctx": k * 2 + core}, device_id_type=MESH
        )
    )
    over_z(lambda k: pl.semaphore_signal(barrier, inc=1, device_id={"ch": k}, device_id_type=MESH))

    loads[0].wait()
    code_row = codes_ref[...]
    onehot[...] = jnp.where(
        lax.broadcasted_iota(jnp.int32, (codes, tokens), 0) == code_row, 1.0, 0.0
    ).astype(BF16)
    loads[1].wait()
    sums[...] = dot(onehot[...], value_ref[...])
    tally[...] = dot(jnp.ones((8, tokens), BF16), onehot[...], NT)[0:1]

    pl.semaphore_wait(barrier, 1 + (chips - 1) + (depth - 1))

    s_core = core_copy(0, sums.at[theirs], sums_x)
    s_core.start()
    t_core = core_copy(1, tally, tally_x)
    t_core.start()

    for load in loads[2:]:
        load.wait()
    norm_row = norm_ref[...]
    weight[...] = jnp.exp(dot(book_ref[...], query_ref[...], NT) * scale - norm_row)
    grads[...] = dot(weight[...].astype(BF16), grad_ref[...])
    g_core = core_copy(2, grads.at[theirs], grads_x)
    g_core.start()

    s_core.wait_recv()
    sums_t[...] = sums[mine] + sums_x[...]
    far_first(lambda k: plane_copy(0, k, sums_t.at[rows(k, piece)], sums_in.at[chip]).start())
    sums_in[chip] = sums_t[rows(chip, piece)]

    g_core.wait_recv()
    grads_t[...] = grads[mine] + grads_x[...]
    grads_in[chip] = grads_t[rows(chip, piece)]

    def grads_part(n, first, size):
        def send(k):
            source = grads_t.at[pl.ds(pl.multiple_of(k * piece + first, 8), size)]
            plane_copy(n, k, source, grads_in.at[chip, pl.ds(first, size)]).start()

        over_plane(send)

    if early:
        grads_part(2, 0, early)

    t_core.wait_recv()
    tally_t[...] = tally[...] + tally_x[...]
    over_plane(lambda k: plane_copy(1, k, tally_t, tally_in.at[chip]).start())
    tally_in[chip] = tally_t[...]

    key_t = dot(book_ref[...].astype(F32).T.astype(BF16), onehot[...]).astype(BF16)
    keys = key_t.astype(F32).T.astype(BF16)
    causal = lax.broadcasted_iota(jnp.int32, (tokens, tokens), 0) <= lax.broadcasted_iota(
        jnp.int32, (tokens, tokens), 1
    )
    in_block = jnp.where(
        causal, jnp.exp(dot(keys, query_ref[...], NT) * scale - norm_row), 0.0
    )
    probs[...] = in_block.astype(BF16)
    product = grad_ref[...].astype(F32) * out_ref[...].astype(F32)
    product_high, product_low = split(product)
    ones = jnp.ones((8, channels), BF16)
    delta = (dot(ones, product_high, NT) + dot(ones, product_low, NT))[0:1]
    dscore = in_block * (dot(value_ref[...], grad_ref[...], NT) - delta)
    dscore_high, dscore_low = split(dscore)
    inner[...] = dot(onehot[...], dscore_high) + dot(onehot[...], dscore_low)

    def plane_bytes(n, ref):
        return plane_copy(n, chip, ref, ref)

    def z_bytes(n, ref):
        return z_copy(n, z, ref, ref)

    def wait_plane(n, buffer):
        plane_bytes(n, buffer.at[pl.ds(0, chips - 1)]).wait_recv()

    def scan(buffer, result, backward):
        def step(i, total):
            k = chips - 1 - i if backward else i
            result[k] = total
            return total + buffer[k]

        lax.fori_loop(0, chips, step, jnp.zeros((piece, channels), F32))

    early_bytes = grads_t.at[pl.ds(0, (chips - 1) * early)]
    late_bytes = grads_t.at[pl.ds(0, (chips - 1) * (piece - early))]
    wait_plane(0, sums_in)
    scan(sums_in, sums_out, False)
    far_first(
        lambda k: plane_copy(3, k, sums_out.at[k], sums_p.at[rows(chip, piece)]).start()
    )
    sums_p[rows(chip, piece)] = sums_out[chip]
    local_values[...] = dot(probs[...], grad_ref[...])

    wait_plane(1, tally_in)

    def count_step(k, total):
        return total + jnp.where(k < chip, 1.0, 0.0) * tally_in[k]

    count = lax.fori_loop(0, chips, count_step, is_one * tally_x[...])
    count_col = jnp.broadcast_to(count, (128, codes)).T[:, 0:1]

    def wait_rows(n, buffer, size):
        plane_bytes(n, buffer.at[pl.ds(0, (chips - 1) * size)]).wait_recv()

    wait_rows(3, sums_p, piece)
    sums_f[...] = sums_p[...] + is_zero * sums[mine]
    s_back = core_copy(3, sums_f, sums_h)
    s_back.start()
    if early < piece:
        grads_part(7, early, piece - early)
    query = query_ref[...]

    def code_grad(cache, span, counts):
        cached = dot(cache, grad_ref[...], NT)
        return split(weight[span] * (cached - counts * delta) + inner[span])

    low_counts, high_counts = count_col[:half], count_col[half:]
    high, low = code_grad(
        (sums_p[...] + is_one * sums_x[...]).astype(BF16),
        mine,
        jnp.where(core == 1, high_counts, low_counts),
    )
    book_p[0] = (dot(high, query) + dot(low, query)) * scale
    book_part = book_ref[mine].astype(F32).T.astype(BF16)
    gq_p[...] = dot(book_part, high) + dot(book_part, low)
    book_part = book_ref[theirs].astype(F32).T.astype(BF16)
    s_back.wait_recv()
    high, low = code_grad(
        sums_h[...].astype(BF16), theirs, jnp.where(core == 1, low_counts, high_counts)
    )
    book_p[1] = (dot(high, query) + dot(low, query)) * scale
    b_core = core_copy(5, book_p.at[1], book_x)
    b_core.start()
    gq_p[...] = (gq_p[...] + dot(book_part, high) + dot(book_part, low)) * scale
    over_z(lambda k: z_copy(0, k, gq_p.at[rows(k, zrows)], gq_in.at[z]).start())
    gq_in[z] = gq_p[rows(z, zrows)]

    b_core.wait_recv()
    book_t[...] = book_p[0] + book_x[...]
    over_plane(lambda k: plane_copy(5, k, book_t.at[rows(k, piece)], book_in.at[chip]).start())
    book_in[chip] = book_t[rows(chip, piece)]

    if early:
        plane_bytes(2, early_bytes).wait_recv()
    if early < piece:
        plane_bytes(7, late_bytes).wait_recv()
    scan(grads_in, grads_out, True)
    over_plane(
        lambda k: plane_copy(4, k, grads_out.at[k], grads_p.at[rows(chip, piece)]).start()
    )
    grads_p[rows(chip, piece)] = grads_out[chip]

    wait_plane(5, book_in)
    book_s[...] = lax.fori_loop(
        0, chips, lambda k, total: total + book_in[k], jnp.zeros((piece, dk), F32)
    )
    over_z(lambda k: z_copy(1, k, book_s, book_z.at[z]).start())
    book_z[z] = book_s[...]

    def wait_z(n, buffer):
        z_bytes(n, buffer.at[pl.ds(0, depth - 1)]).wait_recv()

    wait_z(0, gq_in)
    gq_s[...] = lax.fori_loop(
        0, depth, lambda k, total: total + gq_in[k], jnp.zeros((zrows, tokens), F32)
    )
    over_z(lambda k: z_copy(2, k, gq_s, gq_r.at[rows(z, zrows)]).start())
    gq_r[rows(z, zrows)] = gq_s[...]

    wait_z(1, book_z)
    book_o[...] = lax.fori_loop(
        0, depth, lambda k, total: total + book_z[k], jnp.zeros((piece, dk), F32)
    )
    over_plane(lambda k: plane_copy(6, k, book_o, book_r.at[rows(chip, piece)]).start())
    book_r[rows(chip, piece)] = book_o[...]

    wait_rows(4, grads_p, piece)
    grads_f[...] = grads_p[...] + is_one * grads[mine]
    g_back = core_copy(4, grads_f, grads_h)
    g_back.start()

    own_later = grads_p[...] + is_zero * grads_x[...]
    lookup = onehot[...].T
    low_half = core == 0
    g_back.wait_recv()
    other_later = grads_h[...]
    first = jnp.where(low_half, own_later, other_later)
    second = jnp.where(low_half, other_later, own_later)
    first_high, first_low = split(first)
    second_high, second_low = split(second)
    looked_up = (
        dot(lookup[:, :half], first_high)
        + dot(lookup[:, :half], first_low)
        + dot(lookup[:, half:], second_high)
        + dot(lookup[:, half:], second_low)
    )
    gv_ref[...] = (local_values[...] + looked_up).astype(BF16)

    wait_rows(6, book_r, piece)
    b_back = core_copy(6, book_r, book_h)
    b_back.start()
    z_bytes(2, gq_r.at[pl.ds(0, (depth - 1) * zrows)]).wait_recv()
    gq_ref[...] = gq_r[...].T
    gb_ref[mine] = book_r[...]
    b_back.wait_recv()
    gb_ref[theirs] = book_h[...]

    for copy in (s_core, t_core, g_core, s_back, b_core, g_back, b_back):
        copy.wait_send()

    for n, ref in ((0, sums_in), (1, tally_in), (3, sums_out), (4, grads_out), (5, book_in)):
        plane_bytes(n, ref.at[pl.ds(0, chips - 1)]).wait_send()
    if early:
        plane_bytes(2, early_bytes).wait_send()
    if early < piece:
        plane_bytes(7, late_bytes).wait_send()
    plane_bytes(6, book_r.at[pl.ds(0, (chips - 1) * piece)]).wait_send()
    z_bytes(0, gq_in.at[pl.ds(0, depth - 1)]).wait_send()
    z_bytes(1, book_z.at[pl.ds(0, depth - 1)]).wait_send()
    z_bytes(2, gq_r.at[pl.ds(0, (depth - 1) * zrows)]).wait_send()


def store(gv_ref, gq_ref, gb_ref, gv_hbm, gq_hbm, gb_hbm, sem):
    copies = [
        pltpu.make_async_copy(source, target, sem.at[n])
        for n, (source, target) in enumerate(
            ((gv_ref, gv_hbm), (gq_ref, gq_hbm), (gb_ref, gb_hbm))
        )
    ]
    for copy in copies:
        copy.start()
    for copy in copies:
        copy.wait()


def local(chips, depth, queries, codes, codebook, values, grad_out, attn_out, normalizer):
    tokens, channels = values.shape
    count, dk = codebook.shape
    half = count // 2
    piece = half // chips
    zrows = dk // depth

    def f32(*shape):
        return pltpu.VMEM(shape, F32)

    def scan_scratch():
        return [
            f32(count, channels),
            f32(half, channels),
            f32(half, channels),
            f32(chips, piece, channels),
            f32(chips, piece, channels),
            f32(half, channels),
            f32(half, channels),
            f32(half, channels),
        ]

    scratch = (
        [
            pltpu.VMEM((1, tokens), jnp.int32),
            pltpu.VMEM((tokens, channels), BF16),
            pltpu.VMEM((count, dk), BF16),
            pltpu.VMEM((tokens, dk), BF16),
            f32(1, tokens),
            pltpu.VMEM((tokens, channels), BF16),
            pltpu.VMEM((tokens, channels), BF16),
            pltpu.SemaphoreType.DMA((7,)),
            pltpu.VMEM((count, tokens), BF16),
            f32(count, tokens),
            pltpu.VMEM((tokens, tokens), BF16),
            f32(count, tokens),
            f32(tokens, channels),
        ]
        + scan_scratch()
        + scan_scratch()
        + [f32(1, count), f32(1, count), f32(1, count), f32(chips, 1, count)]
        + [
            f32(2, half, dk),
            f32(half, dk),
            f32(half, dk),
            f32(chips, piece, dk),
            f32(piece, dk),
            f32(depth, piece, dk),
            f32(piece, dk),
            f32(half, dk),
            f32(half, dk),
        ]
        + [f32(dk, tokens), f32(depth, zrows, tokens), f32(zrows, tokens), f32(dk, tokens)]
        + [
            pltpu.SemaphoreType.DMA((8,)),
            pltpu.SemaphoreType.DMA((8,)),
            pltpu.SemaphoreType.DMA((8,)),
            pltpu.SemaphoreType.DMA((8,)),
            pltpu.SemaphoreType.DMA((3,)),
            pltpu.SemaphoreType.DMA((3,)),
        ]
    )
    results = pl.pallas_call(
        functools.partial(kernel, chips, depth),
        out_shape=(
            pltpu.VMEM((tokens, channels), BF16),
            pltpu.VMEM((tokens, dk), F32),
            pltpu.VMEM((count, dk), F32),
        ),
        in_specs=[pl.BlockSpec(memory_space=pltpu.HBM)] * 7,
        out_specs=[pl.BlockSpec(memory_space=pltpu.VMEM)] * 3,
        scratch_shapes=scratch,
        compiler_params=pltpu.CompilerParams(
            collective_id=0, has_side_effects=True, vmem_limit_bytes=60 * 1024 * 1024
        ),
        name="vq_backward",
    )(
        codes.reshape(1, tokens),
        values,
        codebook,
        queries,
        normalizer.reshape(1, tokens),
        grad_out,
        attn_out,
    )
    return pl.pallas_call(
        store,
        out_shape=(
            jax.ShapeDtypeStruct((tokens, channels), BF16),
            jax.ShapeDtypeStruct((tokens, dk), F32),
            jax.ShapeDtypeStruct((count, dk), F32),
        ),
        in_specs=[pl.BlockSpec(memory_space=pl.ANY)] * 3,
        out_specs=[pl.BlockSpec(memory_space=pltpu.HBM)] * 3,
        scratch_shapes=[pltpu.SemaphoreType.DMA((3,))],
        compiler_params=pltpu.CompilerParams(vmem_limit_bytes=4 * 1024 * 1024),
        name="store",
    )(*results)


def solution(mesh):
    in_specs = (
        P("ctx", None),
        P("ctx"),
        P(),
        P("ctx", "ch"),
        P("ctx", "ch"),
        P("ctx", "ch"),
        P("ctx"),
    )
    out_specs = (P("ctx", "ch"), P("ctx", None), P())
    step = functools.partial(local, mesh.shape["ctx"] // 2, mesh.shape["ch"])
    return jax.shard_map(step, mesh=mesh, in_specs=in_specs, out_specs=out_specs, check_vma=False)
```

time: 67.6 us -> 52.4 us (0.78)
  Pallas kernels: 63.1 us -> 51.6 us
  local copies, waits for them, and re-layouts: 3.66 us -> 0 us
    pallas_call x1 -> x2, Pallas kernels: 63.1 us -> 51.6 us  [the longest x1 50.6 us: local(): pl.pallas_call(functools.partial(kernel, chips, depth), out_shape=(pltpu....]
    unnamed x7 -> x0, local copies, waits for them, and re-layouts: 3.66 us -> none
where the time goes in v2:
time: 52.4 us; the launch traced here: 52.3 us
  Pallas kernels  51.6 us (98%)
  between operations  0.64 us (1%)
    pallas_call x1, Pallas kernels, local(): pl.pallas_call(functools.partial(kernel, chips, depth), out_shape=(pltpu....  50.6 us

profile of v2, /device:TPU:1, one launch (start us, length us, event | category | flops | bytes accessed | tf_op | source)
XLA Modules:
  0.0 52.3 jit_solution(11516359289524712253)
XLA Ops:
  0.6 50.6 %vq_backward.1 = (bf16[512,512]{1,0:T(8,128)(2,1)S(1)}, f32[512,128]{1,0:T(8,128)S(1)}, f32[512,128]{1,0:T(8,128)S(1)}) custom-call(s32[1,512]{1,0:T(1,128)} %bitcast.2, bf16[512,512]{1,0:T(8,128)(2,1)} %value_hbm.1, bf16[512,128]{1,0:T(8,128)(2,1)} %book_hbm.1, bf16[512,128]{1,0:T(8,128)(2,1)} %query_hbm.1, f32[1,512]{1,0:T(1,128)} %bitcast.3, ...), custom_call_target="tpu_custom_call" | custom-call | tf_op jit(solution)/shard_map/vq_backward/pallas_call | solution.py:491
  51.3 1.0 %store.1 = (bf16[512,512]{1,0:T(8,128)(2,1)}, f32[512,128]{1,0:T(8,128)}, f32[512,128]{1,0:T(8,128)}) custom-call(bf16[512,512]{1,0:T(8,128)(2,1)S(1)} %get-tuple-element.6.gv_ref, f32[512,128]{1,0:T(8,128)S(1)} %get-tuple-element.7.gq_ref, f32[512,128]{1,0:T(8,128)S(1)} %get-tuple-element.8.gb_ref), custom_call_target="tpu_custom_call" | custom-call | tf_op jit(solution)/shard_map/store/pallas_call | solution.py:514

commit v3 on v2

--- a/solution.py
+++ b/solution.py
@@ -62,8 +62,6 @@
     sums_in,
     sums_out,
     sums_p,
-    sums_f,
-    sums_h,
     grads,
     grads_x,
     grads_t,
@@ -72,12 +70,21 @@
     grads_p,
     grads_f,
     grads_h,
+    query_s,
+    query_x,
+    grad_s,
+    grad_x,
+    grad_o,
+    weight_o,
+    inner_x,
+    norm_x,
+    delta_s,
+    delta_x,
+    lookup,
     tally,
     tally_x,
     tally_t,
     tally_in,
-    book_p,
-    book_x,
     book_t,
     book_in,
     book_s,
@@ -85,6 +92,8 @@
     book_o,
     book_r,
     book_h,
+    gq_o,
+    gq_x,
     gq_p,
     gq_in,
     gq_s,
@@ -160,11 +169,15 @@
             body(lax.rem(y + dy, 4) * 4 + lax.rem(x + dx, 4))
 
     def over_z(body):
+        half_way = depth // 2
+        body(lax.rem(z + half_way, depth))
+
         def step(i, carry):
-            body(lax.rem(z + i, depth))
+            body(lax.rem(z + half_way + i, depth))
+            body(lax.rem(z + half_way - i, depth))
             return carry
 
-        lax.fori_loop(1, depth, step, 0)
+        lax.fori_loop(1, half_way, step, 0)
 
     loads = [
         pltpu.make_async_copy(source, target, load_sem.at[n])
@@ -216,6 +229,12 @@
     g_core = core_copy(2, grads.at[theirs], grads_x)
     g_core.start()
 
+    query_s[...] = query_ref[...].astype(F32)
+    q_core = core_copy(7, query_s, query_x)
+    n_core = core_copy(8, norm_ref, norm_x)
+    q_core.start()
+    n_core.start()
+
     s_core.wait_recv()
     sums_t[...] = sums[mine] + sums_x[...]
     far_first(lambda k: plane_copy(0, k, sums_t.at[rows(k, piece)], sums_in.at[chip]).start())
@@ -230,15 +249,16 @@
             source = grads_t.at[pl.ds(pl.multiple_of(k * piece + first, 8), size)]
             plane_copy(n, k, source, grads_in.at[chip, pl.ds(first, size)]).start()
 
-        over_plane(send)
-
-    if early:
-        grads_part(2, 0, early)
+        far_first(send)
 
     t_core.wait_recv()
     tally_t[...] = tally[...] + tally_x[...]
     over_plane(lambda k: plane_copy(1, k, tally_t, tally_in.at[chip]).start())
     tally_in[chip] = tally_t[...]
+
+    grad_s[...] = grad_ref[...].astype(F32)
+    o_core = core_copy(9, grad_s, grad_x)
+    o_core.start()
 
     key_t = dot(book_ref[...].astype(F32).T.astype(BF16), onehot[...]).astype(BF16)
     keys = key_t.astype(F32).T.astype(BF16)
@@ -253,9 +273,14 @@
     product_high, product_low = split(product)
     ones = jnp.ones((8, channels), BF16)
     delta = (dot(ones, product_high, NT) + dot(ones, product_low, NT))[0:1]
+    delta_s[...] = delta
+    d_core = core_copy(10, delta_s, delta_x)
+    d_core.start()
     dscore = in_block * (dot(value_ref[...], grad_ref[...], NT) - delta)
     dscore_high, dscore_low = split(dscore)
     inner[...] = dot(onehot[...], dscore_high) + dot(onehot[...], dscore_low)
+    i_core = core_copy(5, inner.at[theirs], inner_x)
+    i_core.start()
 
     def plane_bytes(n, ref):
         return plane_copy(n, chip, ref, ref)
@@ -282,63 +307,69 @@
         lambda k: plane_copy(3, k, sums_out.at[k], sums_p.at[rows(chip, piece)]).start()
     )
     sums_p[rows(chip, piece)] = sums_out[chip]
+    if early:
+        grads_part(2, 0, early)
+
     local_values[...] = dot(probs[...], grad_ref[...])
+    lookup[0] = onehot[mine].T
+    lookup[1] = onehot[theirs].T
+
+    q_core.wait_recv()
+    n_core.wait_recv()
+    query_o = query_x[...].astype(BF16)
+    book_half = book_ref[mine]
+    weight_o[...] = jnp.exp(dot(book_half, query_o, NT) * scale - norm_x[...])
+    book_half_t = book_half.astype(F32).T.astype(BF16)
+    o_core.wait_recv()
+    grad_o[...] = grad_x[...].astype(BF16)
 
     wait_plane(1, tally_in)
 
     def count_step(k, total):
         return total + jnp.where(k < chip, 1.0, 0.0) * tally_in[k]
 
-    count = lax.fori_loop(0, chips, count_step, is_one * tally_x[...])
-    count_col = jnp.broadcast_to(count, (128, codes)).T[:, 0:1]
+    count = lax.fori_loop(0, chips, count_step, jnp.zeros((1, codes), F32))
+
+    def half_column(row):
+        column = jnp.broadcast_to(row, (128, codes)).T[:, 0:1]
+        return jnp.where(core == 1, column[half:], column[:half])
+
+    counts = half_column(count + is_one * tally_x[...])
+    counts_o = half_column(count + is_zero * tally[...])
+    i_core.wait_recv()
+    d_core.wait_recv()
 
     def wait_rows(n, buffer, size):
         plane_bytes(n, buffer.at[pl.ds(0, (chips - 1) * size)]).wait_recv()
 
     wait_rows(3, sums_p, piece)
-    sums_f[...] = sums_p[...] + is_zero * sums[mine]
-    s_back = core_copy(3, sums_f, sums_h)
-    s_back.start()
     if early < piece:
         grads_part(7, early, piece - early)
+    cached = dot((sums_p[...] + is_zero * sums[mine]).astype(BF16), grad_o[...], NT)
+    high_o, low_o = split(weight_o[...] * (cached - counts_o * delta_x[...]) + inner_x[...])
+    gq_o[...] = dot(book_half_t, high_o) + dot(book_half_t, low_o)
+    gq_core = core_copy(3, gq_o, gq_x)
+    gq_core.start()
+    cached = dot((sums_p[...] + is_one * sums_x[...]).astype(BF16), grad_ref[...], NT)
+    high, low = split(weight[mine] * (cached - counts * delta) + inner[mine])
     query = query_ref[...]
-
-    def code_grad(cache, span, counts):
-        cached = dot(cache, grad_ref[...], NT)
-        return split(weight[span] * (cached - counts * delta) + inner[span])
-
-    low_counts, high_counts = count_col[:half], count_col[half:]
-    high, low = code_grad(
-        (sums_p[...] + is_one * sums_x[...]).astype(BF16),
-        mine,
-        jnp.where(core == 1, high_counts, low_counts),
-    )
-    book_p[0] = (dot(high, query) + dot(low, query)) * scale
-    book_part = book_ref[mine].astype(F32).T.astype(BF16)
-    gq_p[...] = dot(book_part, high) + dot(book_part, low)
-    book_part = book_ref[theirs].astype(F32).T.astype(BF16)
-    s_back.wait_recv()
-    high, low = code_grad(
-        sums_h[...].astype(BF16), theirs, jnp.where(core == 1, low_counts, high_counts)
-    )
-    book_p[1] = (dot(high, query) + dot(low, query)) * scale
-    b_core = core_copy(5, book_p.at[1], book_x)
-    b_core.start()
-    gq_p[...] = (gq_p[...] + dot(book_part, high) + dot(book_part, low)) * scale
+    book_t[...] = (
+        dot(high_o, query_o) + dot(low_o, query_o) + dot(high, query) + dot(low, query)
+    ) * scale
+    far_first(lambda k: plane_copy(5, k, book_t.at[rows(k, piece)], book_in.at[chip]).start())
+    book_in[chip] = book_t[rows(chip, piece)]
+    own = dot(book_half_t, high) + dot(book_half_t, low)
+    gq_core.wait_recv()
+    gq_p[...] = (own + gq_x[...]) * scale
     over_z(lambda k: z_copy(0, k, gq_p.at[rows(k, zrows)], gq_in.at[z]).start())
     gq_in[z] = gq_p[rows(z, zrows)]
-
-    b_core.wait_recv()
-    book_t[...] = book_p[0] + book_x[...]
-    over_plane(lambda k: plane_copy(5, k, book_t.at[rows(k, piece)], book_in.at[chip]).start())
-    book_in[chip] = book_t[rows(chip, piece)]
 
     if early:
         plane_bytes(2, early_bytes).wait_recv()
     if early < piece:
         plane_bytes(7, late_bytes).wait_recv()
     scan(grads_in, grads_out, True)
-    over_plane(
+    far_first(
         lambda k: plane_copy(4, k, grads_out.at[k], grads_p.at[rows(chip, piece)]).start()
     )
     grads_p[rows(chip, piece)] = grads_out[chip]
@@ -364,30 +395,20 @@
     book_o[...] = lax.fori_loop(
         0, depth, lambda k, total: total + book_z[k], jnp.zeros((piece, dk), F32)
     )
-    over_plane(lambda k: plane_copy(6, k, book_o, book_r.at[rows(chip, piece)]).start())
+    far_first(lambda k: plane_copy(6, k, book_o, book_r.at[rows(chip, piece)]).start())
     book_r[rows(chip, piece)] = book_o[...]
+
+    def look_up(n, rows_later):
+        later_high, later_low = split(rows_later)
+        return dot(lookup[n], later_high) + dot(lookup[n], later_low)
 
     wait_rows(4, grads_p, piece)
     grads_f[...] = grads_p[...] + is_one * grads[mine]
     g_back = core_copy(4, grads_f, grads_h)
     g_back.start()
-
-    own_later = grads_p[...] + is_zero * grads_x[...]
-    lookup = onehot[...].T
-    low_half = core == 0
+    local_values[...] += look_up(0, grads_p[...] + is_zero * grads_x[...])
     g_back.wait_recv()
-    other_later = grads_h[...]
-    first = jnp.where(low_half, own_later, other_later)
-    second = jnp.where(low_half, other_later, own_later)
-    first_high, first_low = split(first)
-    second_high, second_low = split(second)
-    looked_up = (
-        dot(lookup[:, :half], first_high)
-        + dot(lookup[:, :half], first_low)
-        + dot(lookup[:, half:], second_high)
-        + dot(lookup[:, half:], second_low)
-    )
-    gv_ref[...] = (local_values[...] + looked_up).astype(BF16)
+    gv_ref[...] = (local_values[...] + look_up(1, grads_h[...])).astype(BF16)
 
     wait_rows(6, book_r, piece)
     b_back = core_copy(6, book_r, book_h)
@@ -398,7 +419,10 @@
     b_back.wait_recv()
     gb_ref[theirs] = book_h[...]
 
-    for copy in (s_core, t_core, g_core, s_back, b_core, g_back, b_back):
+    for copy in (
+        (s_core, t_core, g_core, q_core, n_core, o_core, d_core, i_core)
+        + (gq_core, g_back, b_back)
+    ):
         copy.wait_send()
 
     for n, ref in ((0, sums_in), (1, tally_in), (3, sums_out), (4, grads_out), (5, book_in)):
@@ -443,8 +467,6 @@
             f32(half, channels),
             f32(chips, piece, channels),
             f32(chips, piece, channels),
-            f32(half, channels),
-            f32(half, channels),
             f32(half, channels),
         ]
 
@@ -466,10 +488,22 @@
         ]
         + scan_scratch()
         + scan_scratch()
+        + [f32(half, channels), f32(half, channels)]
+        + [
+            f32(tokens, dk),
+            f32(tokens, dk),
+            f32(tokens, channels),
+            f32(tokens, channels),
+            pltpu.VMEM((tokens, channels), BF16),
+            f32(half, tokens),
+            f32(half, tokens),
+            f32(1, tokens),
+            f32(1, tokens),
+            f32(1, tokens),
+            pltpu.VMEM((2, tokens, half), BF16),
+        ]
         + [f32(1, count), f32(1, count), f32(1, count), f32(chips, 1, count)]
         + [
-            f32(2, half, dk),
-            f32(half, dk),
             f32(half, dk),
             f32(chips, piece, dk),
             f32(piece, dk),
@@ -478,10 +512,10 @@
             f32(half, dk),
             f32(half, dk),
         ]
-        + [f32(dk, tokens), f32(depth, zrows, tokens), f32(zrows, tokens), f32(dk, tokens)]
+        + [f32(dk, tokens), f32(dk, tokens), f32(dk, tokens), f32(depth, zrows, tokens), f32(zrows, tokens), f32(dk, tokens)]
         + [
-            pltpu.SemaphoreType.DMA((8,)),
-            pltpu.SemaphoreType.DMA((8,)),
+            pltpu.SemaphoreType.DMA((11,)),
+            pltpu.SemaphoreType.DMA((11,)),
             pltpu.SemaphoreType.DMA((8,)),
             pltpu.SemaphoreType.DMA((8,)),
             pltpu.SemaphoreType.DMA((3,)),

time: 52.4 us -> 50.8 us (0.969)
  Pallas kernels: 51.6 us -> 50.1 us
    pallas_call x1, Pallas kernels: 50.6 us -> 49.1 us  [local(): pl.pallas_call(functools.partial(kernel, chips, depth), out_shape=(pltpu....]
where the time goes in v3:
time: 50.8 us; the launch traced here: 50.7 us
  Pallas kernels  50.1 us (99%)
  between operations  0.64 us (1%)
    pallas_call x1, Pallas kernels, local(): pl.pallas_call(functools.partial(kernel, chips, depth), out_shape=(pltpu....  49.1 us

profile of v3, /device:TPU:1, one launch (start us, length us, event | category | flops | bytes accessed | tf_op | source)
XLA Modules:
  0.0 50.7 jit_solution(13066846351295418)
XLA Ops:
  0.6 49.1 %vq_backward.1 = (bf16[512,512]{1,0:T(8,128)(2,1)S(1)}, f32[512,128]{1,0:T(8,128)S(1)}, f32[512,128]{1,0:T(8,128)S(1)}) custom-call(s32[1,512]{1,0:T(1,128)} %bitcast.2, bf16[512,512]{1,0:T(8,128)(2,1)} %value_hbm.1, bf16[512,128]{1,0:T(8,128)(2,1)} %book_hbm.1, bf16[512,128]{1,0:T(8,128)(2,1)} %query_hbm.1, f32[1,512]{1,0:T(1,128)} %bitcast.3, ...), custom_call_target="tpu_custom_call" | custom-call | tf_op jit(solution)/shard_map/vq_backward/pallas_call | solution.py:525
  49.7 1.0 %store.1 = (bf16[512,512]{1,0:T(8,128)(2,1)}, f32[512,128]{1,0:T(8,128)}, f32[512,128]{1,0:T(8,128)}) custom-call(bf16[512,512]{1,0:T(8,128)(2,1)S(1)} %get-tuple-element.6.gv_ref, f32[512,128]{1,0:T(8,128)S(1)} %get-tuple-element.7.gq_ref, f32[512,128]{1,0:T(8,128)S(1)} %get-tuple-element.8.gb_ref), custom_call_target="tpu_custom_call" | custom-call | tf_op jit(solution)/shard_map/store/pallas_call | solution.py:548

commit v4 on v3

--- a/solution.py
+++ b/solution.py
@@ -8,7 +8,6 @@
 from jax.sharding import PartitionSpec as P
 
 MESH = pl.DeviceIdType.MESH
-EARLY = 8
 F32 = jnp.float32
 BF16 = jnp.bfloat16
 
@@ -91,7 +90,6 @@
     book_z,
     book_o,
     book_r,
-    book_h,
     gq_o,
     gq_x,
     gq_p,
@@ -110,7 +108,9 @@
     half = codes // 2
     piece = half // chips
     zrows = dk // depth
-    early = EARLY
+    quarter = half // 2
+    part = piece // 2
+    parts = (pl.ds(0, quarter), pl.ds(quarter, quarter))
     scale = float(dk) ** -0.5
 
     ctx = lax.axis_index("ctx")
@@ -143,6 +143,16 @@
             send_sem=plane_send.at[n],
             recv_sem=plane_recv.at[n],
             device_id={"ctx": k * 2 + core},
+            device_id_type=MESH,
+        )
+
+    def cross_copy(k, src, dst):
+        return pltpu.make_async_remote_copy(
+            src_ref=src,
+            dst_ref=dst,
+            send_sem=plane_send.at[9],
+            recv_sem=plane_recv.at[9],
+            device_id={"ctx": k * 2 + (1 - core)},
             device_id_type=MESH,
         )
 
@@ -198,11 +208,12 @@
 
     barrier = pltpu.get_barrier_semaphore()
     pl.semaphore_signal(barrier, inc=1, device_id={"ctx": other}, device_id_type=MESH)
-    over_plane(
-        lambda k: pl.semaphore_signal(
-            barrier, inc=1, device_id={"ctx": k * 2 + core}, device_id_type=MESH
-        )
-    )
+
+    def greet(k):
+        for index in (k * 2, k * 2 + 1):
+            pl.semaphore_signal(barrier, inc=1, device_id={"ctx": index}, device_id_type=MESH)
+
+    over_plane(greet)
     over_z(lambda k: pl.semaphore_signal(barrier, inc=1, device_id={"ch": k}, device_id_type=MESH))
 
     loads[0].wait()
@@ -214,7 +225,7 @@
     sums[...] = dot(onehot[...], value_ref[...])
     tally[...] = dot(jnp.ones((8, tokens), BF16), onehot[...], NT)[0:1]
 
-    pl.semaphore_wait(barrier, 1 + (chips - 1) + (depth - 1))
+    pl.semaphore_wait(barrier, 1 + 2 * (chips - 1) + (depth - 1))
 
     s_core = core_copy(0, sums.at[theirs], sums_x)
     s_core.start()
@@ -227,27 +238,27 @@
     weight[...] = jnp.exp(dot(book_ref[...], query_ref[...], NT) * scale - norm_row)
     grads[...] = dot(weight[...].astype(BF16), grad_ref[...])
     g_core = core_copy(2, grads.at[theirs], grads_x)
-    g_core.start()
 
     query_s[...] = query_ref[...].astype(F32)
     q_core = core_copy(7, query_s, query_x)
     n_core = core_copy(8, norm_ref, norm_x)
-    q_core.start()
-    n_core.start()
 
     s_core.wait_recv()
     sums_t[...] = sums[mine] + sums_x[...]
     far_first(lambda k: plane_copy(0, k, sums_t.at[rows(k, piece)], sums_in.at[chip]).start())
+    for copy in (g_core, q_core, n_core):
+        copy.start()
     sums_in[chip] = sums_t[rows(chip, piece)]
 
     g_core.wait_recv()
     grads_t[...] = grads[mine] + grads_x[...]
-    grads_in[chip] = grads_t[rows(chip, piece)]
-
-    def grads_part(n, first, size):
+    for n in (0, 1):
+        grads_in[n, chip] = grads_t[pl.ds(pl.multiple_of(n * quarter + chip * part, part), part)]
+
+    def grads_send(n):
         def send(k):
-            source = grads_t.at[pl.ds(pl.multiple_of(k * piece + first, 8), size)]
-            plane_copy(n, k, source, grads_in.at[chip, pl.ds(first, size)]).start()
+            source = grads_t.at[pl.ds(pl.multiple_of(n * quarter + k * part, part), part)]
+            plane_copy((2, 7)[n], k, source, grads_in.at[n, chip]).start()
 
         far_first(send)
 
@@ -297,19 +308,26 @@
             result[k] = total
             return total + buffer[k]
 
-        lax.fori_loop(0, chips, step, jnp.zeros((piece, channels), F32))
-
-    early_bytes = grads_t.at[pl.ds(0, (chips - 1) * early)]
-    late_bytes = grads_t.at[pl.ds(0, (chips - 1) * (piece - early))]
+        lax.fori_loop(0, chips, step, jnp.zeros(buffer.shape[1:], F32))
+
+    part_bytes = grads_t.at[pl.ds(0, (chips - 1) * part)]
+
+    def grads_scan(n):
+        plane_bytes((2, 7)[n], part_bytes).wait_recv()
+        scan(grads_in.at[n], grads_out.at[n], True)
+        place = pl.ds(pl.multiple_of(n * quarter + chip * part, part), part)
+        far_first(
+            lambda k: plane_copy((4, 8)[n], k, grads_out.at[n, k], grads_p.at[place]).start()
+        )
+        grads_p[place] = grads_out[n, chip]
+
     wait_plane(0, sums_in)
     scan(sums_in, sums_out, False)
     far_first(
         lambda k: plane_copy(3, k, sums_out.at[k], sums_p.at[rows(chip, piece)]).start()
     )
     sums_p[rows(chip, piece)] = sums_out[chip]
-    if early:
-        grads_part(2, 0, early)
-
+    grads_send(0)
     local_values[...] = dot(probs[...], grad_ref[...])
     lookup[0] = onehot[mine].T
     lookup[1] = onehot[theirs].T
@@ -343,8 +361,7 @@
         plane_bytes(n, buffer.at[pl.ds(0, (chips - 1) * size)]).wait_recv()
 
     wait_rows(3, sums_p, piece)
-    if early < piece:
-        grads_part(7, early, piece - early)
+    grads_send(1)
     cached = dot((sums_p[...] + is_zero * sums[mine]).astype(BF16), grad_o[...], NT)
     high_o, low_o = split(weight_o[...] * (cached - counts_o * delta_x[...]) + inner_x[...])
     gq_o[...] = dot(book_half_t, high_o) + dot(book_half_t, low_o)
@@ -364,15 +381,8 @@
     over_z(lambda k: z_copy(0, k, gq_p.at[rows(k, zrows)], gq_in.at[z]).start())
     gq_in[z] = gq_p[rows(z, zrows)]
 
-    if early:
-        plane_bytes(2, early_bytes).wait_recv()
-    if early < piece:
-        plane_bytes(7, late_bytes).wait_recv()
-    scan(grads_in, grads_out, True)
-    far_first(
-        lambda k: plane_copy(4, k, grads_out.at[k], grads_p.at[rows(chip, piece)]).start()
-    )
-    grads_p[rows(chip, piece)] = grads_out[chip]
+    grads_scan(0)
+    grads_scan(1)
 
     wait_plane(5, book_in)
     book_s[...] = lax.fori_loop(
@@ -395,43 +405,58 @@
     book_o[...] = lax.fori_loop(
         0, depth, lambda k, total: total + book_z[k], jnp.zeros((piece, dk), F32)
     )
-    far_first(lambda k: plane_copy(6, k, book_o, book_r.at[rows(chip, piece)]).start())
-    book_r[rows(chip, piece)] = book_o[...]
-
-    def look_up(n, rows_later):
+    place = pl.ds(pl.multiple_of(core * half + chip * piece, piece), piece)
+
+    def book_send(k):
+        plane_copy(6, k, book_o, book_r.at[place]).start()
+        cross_copy(k, book_o, book_r.at[place]).start()
+
+    far_first(book_send)
+    b_back = core_copy(6, book_o, book_r.at[place])
+    b_back.start()
+    book_r[place] = book_o[...]
+
+    def look_up(which, n, rows_later):
         later_high, later_low = split(rows_later)
-        return dot(lookup[n], later_high) + dot(lookup[n], later_low)
-
-    wait_rows(4, grads_p, piece)
-    grads_f[...] = grads_p[...] + is_one * grads[mine]
-    g_back = core_copy(4, grads_f, grads_h)
-    g_back.start()
-    local_values[...] += look_up(0, grads_p[...] + is_zero * grads_x[...])
+        table = lookup[which, :, parts[n]]
+        return dot(table, later_high) + dot(table, later_low)
+
+    def grads_back(n):
+        plane_bytes((4, 8)[n], part_bytes).wait_recv()
+        own = pl.ds(pl.multiple_of(core * half + n * quarter, quarter), quarter)
+        grads_f[parts[n]] = grads_p[parts[n]] + is_one * grads[own]
+        back = core_copy((4, 11)[n], grads_f.at[parts[n]], grads_h.at[parts[n]])
+        back.start()
+        local_values[...] += look_up(0, n, grads_p[parts[n]] + is_zero * grads_x[parts[n]])
+        return back
+
+    g_back = grads_back(0)
+    g_back_late = grads_back(1)
     g_back.wait_recv()
-    gv_ref[...] = (local_values[...] + look_up(1, grads_h[...])).astype(BF16)
-
-    wait_rows(6, book_r, piece)
-    b_back = core_copy(6, book_r, book_h)
-    b_back.start()
+    local_values[...] += look_up(1, 0, grads_h[parts[0]])
+    g_back_late.wait_recv()
+    gv_ref[...] = (local_values[...] + look_up(1, 1, grads_h[parts[1]])).astype(BF16)
+
     z_bytes(2, gq_r.at[pl.ds(0, (depth - 1) * zrows)]).wait_recv()
     gq_ref[...] = gq_r[...].T
-    gb_ref[mine] = book_r[...]
+    book_bytes = book_r.at[pl.ds(0, (chips - 1) * piece)]
+    plane_bytes(6, book_bytes).wait_recv()
+    cross_copy(chip, book_bytes, book_bytes).wait_recv()
     b_back.wait_recv()
-    gb_ref[theirs] = book_h[...]
+    gb_ref[...] = book_r[...]
 
     for copy in (
         (s_core, t_core, g_core, q_core, n_core, o_core, d_core, i_core)
-        + (gq_core, g_back, b_back)
+        + (gq_core, g_back, g_back_late, b_back)
     ):
         copy.wait_send()
 
-    for n, ref in ((0, sums_in), (1, tally_in), (3, sums_out), (4, grads_out), (5, book_in)):
+    for n, ref in ((0, sums_in), (1, tally_in), (3, sums_out), (5, book_in)):
         plane_bytes(n, ref.at[pl.ds(0, chips - 1)]).wait_send()
-    if early:
-        plane_bytes(2, early_bytes).wait_send()
-    if early < piece:
-        plane_bytes(7, late_bytes).wait_send()
-    plane_bytes(6, book_r.at[pl.ds(0, (chips - 1) * piece)]).wait_send()
+    for n in (2, 7, 4, 8):
+        plane_bytes(n, part_bytes).wait_send()
+    plane_bytes(6, book_bytes).wait_send()
+    cross_copy(chip, book_bytes, book_bytes).wait_send()
     z_bytes(0, gq_in.at[pl.ds(0, depth - 1)]).wait_send()
     z_bytes(1, book_z.at[pl.ds(0, depth - 1)]).wait_send()
     z_bytes(2, gq_r.at[pl.ds(0, (depth - 1) * zrows)]).wait_send()
@@ -460,13 +485,13 @@
     def f32(*shape):
         return pltpu.VMEM(shape, F32)
 
-    def scan_scratch():
+    def scan_scratch(*cut):
         return [
             f32(count, channels),
             f32(half, channels),
             f32(half, channels),
-            f32(chips, piece, channels),
-            f32(chips, piece, channels),
+            f32(*cut, channels),
+            f32(*cut, channels),
             f32(half, channels),
         ]
 
@@ -486,8 +511,8 @@
             f32(count, tokens),
             f32(tokens, channels),
         ]
-        + scan_scratch()
-        + scan_scratch()
+        + scan_scratch(chips, piece)
+        + scan_scratch(2, chips, piece // 2)
         + [f32(half, channels), f32(half, channels)]
         + [
             f32(tokens, dk),
@@ -509,15 +534,14 @@
             f32(piece, dk),
             f32(depth, piece, dk),
             f32(piece, dk),
-            f32(half, dk),
-            f32(half, dk),
+            f32(count, dk),
         ]
         + [f32(dk, tokens), f32(dk, tokens), f32(dk, tokens), f32(depth, zrows, tokens), f32(zrows, tokens), f32(dk, tokens)]
         + [
-            pltpu.SemaphoreType.DMA((11,)),
-            pltpu.SemaphoreType.DMA((11,)),
-            pltpu.SemaphoreType.DMA((8,)),
-            pltpu.SemaphoreType.DMA((8,)),
+            pltpu.SemaphoreType.DMA((12,)),
+            pltpu.SemaphoreType.DMA((12,)),
+            pltpu.SemaphoreType.DMA((10,)),
+            pltpu.SemaphoreType.DMA((10,)),
             pltpu.SemaphoreType.DMA((3,)),
             pltpu.SemaphoreType.DMA((3,)),
         ]

time: 50.8 us -> 51 us (level)
  no operation moved by 1% of the time
where the time goes in v4:
time: 51 us; the launch traced here: 50.9 us
  Pallas kernels  50.3 us (99%)
  between operations  0.64 us (1%)
    pallas_call x1, Pallas kernels, local(): pl.pallas_call(functools.partial(kernel, chips, depth), out_shape=(pltpu....  49.3 us

profile of v4, /device:TPU:1, one launch (start us, length us, event | category | flops | bytes accessed | tf_op | source)
XLA Modules:
  0.0 50.9 jit_solution(14442339826985014917)
XLA Ops:
  0.6 49.3 %vq_backward.1 = (bf16[512,512]{1,0:T(8,128)(2,1)S(1)}, f32[512,128]{1,0:T(8,128)S(1)}, f32[512,128]{1,0:T(8,128)S(1)}) custom-call(s32[1,512]{1,0:T(1,128)} %bitcast.2, bf16[512,512]{1,0:T(8,128)(2,1)} %value_hbm.1, bf16[512,128]{1,0:T(8,128)(2,1)} %book_hbm.1, bf16[512,128]{1,0:T(8,128)(2,1)} %query_hbm.1, f32[1,512]{1,0:T(1,128)} %bitcast.3, ...), custom_call_target="tpu_custom_call" | custom-call | tf_op jit(solution)/shard_map/vq_backward/pallas_call | solution.py:549
  49.9 1.0 %store.1 = (bf16[512,512]{1,0:T(8,128)(2,1)}, f32[512,128]{1,0:T(8,128)}, f32[512,128]{1,0:T(8,128)}) custom-call(bf16[512,512]{1,0:T(8,128)(2,1)S(1)} %get-tuple-element.6.gv_ref, f32[512,128]{1,0:T(8,128)S(1)} %get-tuple-element.7.gq_ref, f32[512,128]{1,0:T(8,128)S(1)} %get-tuple-element.8.gb_ref), custom_call_target="tpu_custom_call" | custom-call | tf_op jit(solution)/shard_map/store/pallas_call | solution.py:572
